TPU v7x, 32 devices: a whole 2x2x4 slice. The times are simulated.
32 devices in a mesh: groups: 2 (over y), ha: 8 (over z, x), wa: 2 (over core).
Axes of the slice: x: 2, y: 2, z: 4, core: 2. Of those that a mesh axis runs over, the one named last changes fastest.
Arguments:
- frames_in: float32 [12, 32, 96, 256], P(None, ('groups', 'ha'), None, 'wa'), parts along dimension 1, may hold values from -6 to 6
- clip_frames: int32 [16], P('groups'), parts along dimension 0, may hold values from 2 to 12, as said below
- conv_weight: float32 [4, 3, 3, 3, 96, 96], replicated, may hold values from -0.125 to 0.125
- conv_bias: float32 [4, 96], replicated, may hold values from -3 to 3
- norm_gain: float32 [4, 96], replicated, may hold values from 0.1 to 1.9
Outputs:
- frames_out: float32 [12, 32, 96, 256], P(None, ('groups', 'ha'), None, 'wa'), parts along dimension 1
There are 2 independent parts, one for each index of `groups`. A program takes and returns all parts, laid end to end along the dimension named above; an argument that names none is the same for every part. Nothing has to cross between parts.
Inputs may be any that keep to these rules, and one draw needn't show every extreme that they name: `clip_frames`: the 4 entries of one slab (indices s * 4 + 4 // 2 onward, modulo 8) are equal; some slab holds 12 frames.
All inputs are finite; a program needn't handle non-finite values.
Results may differ from a plain program's by a relative error of at most 0.0001.
Values sent between devices are 32-bit elements; how exact they have to be, the bound alone decides.
A program may use at most 128 MiB of HBM per device.

v0:
```python
import jax
import jax.numpy as jnp
from jax import lax
from jax.sharding import PartitionSpec as P

SPAN = 4
SLAB_DEVS = 4
BLOCKS = 2


EPS = 1e-06


def extended(cells, sides, width):
    for axis, dim in sides:
        count = lax.axis_size(axis)
        head = lax.slice_in_dim(cells, 0, width, axis=dim)
        tail = lax.slice_in_dim(cells, cells.shape[dim] - width, cells.shape[dim], axis=dim)
        cells = jnp.concatenate(
            [
                lax.ppermute(tail, axis, [(i, (i + 1) % count) for i in range(count)]),
                cells,
                lax.ppermute(head, axis, [((i + 1) % count, i) for i in range(count)]),
            ],
            axis=dim,
        )
    return cells


def activate(field, gain):
    scale = lax.rsqrt(jnp.mean(field * field, axis=-2, keepdims=True) + EPS)
    return jax.nn.silu(field * scale * gain[:, None])


def convolve(padded, weight, bias):
    frames = padded.shape[0] - 2
    length = padded.shape[1] - 2
    width = padded.shape[3] - 2
    total = jnp.zeros((frames, length, weight.shape[3], width), jnp.float32) + bias[:, None]
    for tap_t in range(3):
        for tap_y in range(3):
            for tap_x in range(3):
                piece = padded[
                    tap_t : tap_t + frames, tap_y : tap_y + length, :, tap_x : tap_x + width
                ]
                total = total + jnp.einsum(
                    "frcw,dc->frdw",
                    piece,
                    weight[tap_t, tap_y, tap_x],
                    precision=lax.Precision.HIGHEST,
                )
    return total


def inside(count, offset, base, limit):
    where_at = base + jnp.arange(count, dtype=jnp.int32) - offset
    return (where_at >= 0) & (where_at < limit)


def per_device(frames_in, clip_frames, conv_weight, conv_bias, norm_gain):
    frames, rows, chans, cols = frames_in.shape
    ha_size = lax.axis_size("ha")
    ha_index = lax.axis_index("ha")
    wa_index = lax.axis_index("wa")
    image_cols = lax.axis_size("wa") * cols
    slab_rows = SLAB_DEVS * rows
    row_base = jnp.mod(ha_index - SLAB_DEVS // 2, SLAB_DEVS) * rows
    col_base = wa_index * cols
    spans = frames // SPAN
    slots = jnp.arange(ha_size, dtype=jnp.int32)
    mine = jnp.sum(jnp.where(slots == ha_index, clip_frames, 0))
    mine_spans = (mine + SPAN - 1) // SPAN
    empty = jnp.zeros((SPAN, rows, chans, cols), jnp.float32)

    def conv_layer(field, weight, bias):
        wide = extended(field, (("ha", 1), ("wa", 3)), 1)
        keep_rows = inside(rows + 2, 1, row_base, slab_rows)
        keep_cols = inside(cols + 2, 1, col_base, image_cols)
        keep = keep_rows[None, :, None, None] & keep_cols[None, None, None, :]
        wide = jnp.where(keep, wide, 0.0)
        wide = jnp.pad(wide, ((2, 0), (0, 0), (0, 0), (0, 0)))
        results = []
        for span in range(spans):
            piece = wide[span * SPAN : span * SPAN + SPAN + 2]
            results.append(
                lax.cond(
                    span < mine_spans, lambda p: convolve(p, weight, bias), lambda p: empty, piece
                )
            )
        return jnp.concatenate(results, axis=0)

    field = frames_in
    for block in range(BLOCKS):
        first = 2 * block
        middle = conv_layer(activate(field, norm_gain[first]), conv_weight[first], conv_bias[first])
        field = field + conv_layer(
            activate(middle, norm_gain[first + 1]), conv_weight[first + 1], conv_bias[first + 1]
        )
    live = jnp.arange(frames, dtype=jnp.int32) < mine
    return jnp.where(live[:, None, None, None], field, 0.0)


def solution(mesh):
    placed = (P(None, ("groups", "ha"), None, "wa"), P("groups"), P(), P(), P())
    return jax.shard_map(
        per_device,
        mesh=mesh,
        in_specs=placed,
        out_specs=P(None, ("groups", "ha"), None, "wa"),
        check_vma=False,
    )
```

profile of v0, /device:TPU:5, one launch (start us, length us, event | category | flops | bytes accessed | tf_op | source)
XLA Modules:
  0.0 457.1 jit_solution(240029036952578347)
XLA Ops:
  6.8 3.0 collective-permute-start.1
  10.5 4.6 slice_bitcast_fusion.3
  15.1 16.7 %collective-permute-done = f32[12,1,96,128]{3,2,1,0:T(8,128)S(1)} collective-permute-done((f32[12,1,96,128]{3,2,1,0:T(8,128)}, f32[12,1,96,128]{3,2,1,0:T(8,128)S(1)}, u32[]{:S(2)}, u32[]{:S(2)}) %collective-permute-start) | collective-permute-done | bytes 589856 | tf_op jit(solution)/shard_map/ppermute | solution.py:21
  34.9 3.0 fusion.1121
  37.9 2.6 copy.33
  40.5 2.6 copy.34
  50.9 6.0 %maximum_select_fusion = f32[12,4,96,130]{3,2,1,0:T(8,128)} fusion(f32[12,4,96,1]{3,2,1,0:T(8,128)} %copy.36, f32[12,1,96,128]{3,2,1,0:T(8,128)} %collective-permute-done.1, f32[12,2,96,128]{3,2,1,0:T(8,128)S(1)} %divide_multiply_fusion.3, f32[12,1,96,128]{3,2,1,0:T(8,128)S(1)} %collective-permute-done, f32[12,4,96,1]{3,2,1,0:T(8,128)} %copy.35, ...), kind=kLoop, calls=%fused_computation.1512 | loop fusion | flops 2995200 | bytes 4792840 | tf_op jit(solution)/shard_map/jit(_where)/select_n | solution.py:80
  56.9 22.5 %conditional.14 = (f32[4,2,96,128]{3,2,1,0:T(8,128)S(1)}) conditional(s32[]{:T(128)} %convert_element_type.13, () %tuple.82, (f32[1,96]{1,0:T(1,128)S(1)}, f32[3,3,3,96,96]{4,3,2,1,0:T(8,128)}, f32[12,4,96,130]{3,2,1,0:T(8,128)}) %tuple.98), branch_computations={%region_6.7_spmd, %region_7.8_spmd} | conditional | flops 3060301824 | bytes 46350784 | solution.py:86
  79.4 22.1 %conditional.13 = (f32[4,2,96,128]{3,2,1,0:T(8,128)S(1)}) conditional(s32[]{:T(128)} %convert_element_type.12, () %tuple.80, (f32[1,96]{1,0:T(1,128)S(1)}, f32[3,3,3,96,96]{4,3,2,1,0:T(8,128)}, f32[12,4,96,130]{3,2,1,0:T(8,128)}) %tuple.98), branch_computations={%region_4.5_spmd, %region_5.6_spmd} | conditional | flops 3060301824 | bytes 46350784 | solution.py:86
  101.6 17.1 %conditional.12 = (f32[4,2,96,128]{3,2,1,0:T(8,128)S(1)}) conditional(s32[]{:T(128)} %convert_element_type.11, () %tuple.78, (f32[1,96]{1,0:T(1,128)S(1)}, f32[12,4,96,130]{3,2,1,0:T(8,128)}, f32[3,3,3,96,96]{4,3,2,1,0:T(8,128)}) %tuple.79), branch_computations={%region_2.3_spmd, %region_3.4_spmd} | conditional | flops 3060301824 | bytes 121885120 | solution.py:86
  121.0 4.1 collective-permute-start.5
  125.1 20.9 %collective-permute-done.4 = f32[12,1,96,128]{3,2,1,0:T(8,128)S(1)} collective-permute-done((f32[12,1,96,128]{3,2,1,0:T(8,128)S(1)}, f32[12,1,96,128]{3,2,1,0:T(8,128)S(1)}, u32[]{:S(2)}, u32[]{:S(2)}) %collective-permute-start.4) | collective-permute-done | bytes 589856 | tf_op jit(solution)/shard_map/ppermute | solution.py:21
  149.0 3.0 fusion.1120
  163.1 6.0 %maximum_select_fusion.1 = f32[12,4,96,130]{3,2,1,0:T(8,128)} fusion(f32[12,4,96,1]{3,2,1,0:T(8,128)} %copy.40, f32[12,1,96,128]{3,2,1,0:T(8,128)} %copy-done.31, f32[12,2,96,128]{3,2,1,0:T(8,128)S(1)} %divide_multiply_fusion.2, f32[12,1,96,128]{3,2,1,0:T(8,128)S(1)} %collective-permute-done.4, f32[12,4,96,1]{3,2,1,0:T(8,128)} %copy.39, ...), kind=kLoop, calls=%fused_computation.1513 | loop fusion | flops 2995200 | bytes 4792840 | tf_op jit(solution)/shard_map/jit(_where)/select_n | solution.py:80
  169.1 22.5 %conditional.17 = (f32[4,2,96,128]{3,2,1,0:T(8,128)S(1)}) conditional(s32[]{:T(128)} %convert_element_type.13, () %tuple.86, (f32[1,96]{1,0:T(1,128)S(1)}, f32[3,3,3,96,96]{4,3,2,1,0:T(8,128)}, f32[12,4,96,130]{3,2,1,0:T(8,128)}) %tuple.101), branch_computations={%region_13.14_spmd, %region_14.15_spmd} | conditional | flops 3060301824 | bytes 46350784 | solution.py:86
  191.6 22.5 %conditional.16 = (f32[4,2,96,128]{3,2,1,0:T(8,128)S(1)}) conditional(s32[]{:T(128)} %convert_element_type.12, () %tuple.84, (f32[1,96]{1,0:T(1,128)S(1)}, f32[3,3,3,96,96]{4,3,2,1,0:T(8,128)}, f32[12,4,96,130]{3,2,1,0:T(8,128)}) %tuple.101), branch_computations={%region_11.12_spmd, %region_12.13_spmd} | conditional | flops 3060301824 | bytes 46350784 | solution.py:86
  214.2 17.8 %conditional.15 = (f32[4,2,96,128]{3,2,1,0:T(8,128)}) conditional(s32[]{:T(128)} %convert_element_type.11, () %tuple.77, (f32[1,96]{1,0:T(1,128)S(1)}, f32[12,4,96,130]{3,2,1,0:T(8,128)}, f32[3,3,3,96,96]{4,3,2,1,0:T(8,128)}) %tuple.83), branch_computations={%region_9.10_spmd, %region_10.11_spmd} | conditional | flops 3060301824 | bytes 121885120 | solution.py:86
  233.9 4.1 collective-permute-start.9
  238.1 20.7 %collective-permute-done.8 = f32[12,1,96,128]{3,2,1,0:T(8,128)S(1)} collective-permute-done((f32[12,1,96,128]{3,2,1,0:T(8,128)S(1)}, f32[12,1,96,128]{3,2,1,0:T(8,128)S(1)}, u32[]{:S(2)}, u32[]{:S(2)}) %collective-permute-start.8) | collective-permute-done | bytes 589856 | tf_op jit(solution)/shard_map/ppermute | solution.py:21
  261.8 3.0 fusion.1119
  276.0 6.2 %maximum_select_fusion.2 = f32[12,4,96,130]{3,2,1,0:T(8,128)} fusion(f32[12,4,96,1]{3,2,1,0:T(8,128)} %copy.44, f32[12,1,96,128]{3,2,1,0:T(8,128)} %copy-done.32, f32[12,2,96,128]{3,2,1,0:T(8,128)} %copy-done.20, f32[12,1,96,128]{3,2,1,0:T(8,128)S(1)} %collective-permute-done.8, f32[12,4,96,1]{3,2,1,0:T(8,128)} %copy.43, ...), kind=kLoop, calls=%fused_computation.1514 | loop fusion | flops 2995200 | bytes 4792840 | tf_op jit(solution)/shard_map/jit(_where)/select_n | solution.py:80
  282.2 21.2 %conditional.20 = (f32[4,2,96,128]{3,2,1,0:T(8,128)S(1)}) conditional(s32[]{:T(128)} %convert_element_type.13, () %tuple.92, (f32[1,96]{1,0:T(1,128)S(1)}, f32[3,3,3,96,96]{4,3,2,1,0:T(8,128)S(1)}, f32[12,4,96,130]{3,2,1,0:T(8,128)}) %tuple.104), branch_computations={%region_20.21_spmd, %region_21.22_spmd} | conditional | flops 3060301824 | bytes 42369572 | solution.py:86
  303.4 21.3 %conditional.19 = (f32[4,2,96,128]{3,2,1,0:T(8,128)S(1)}) conditional(s32[]{:T(128)} %convert_element_type.12, () %tuple.90, (f32[1,96]{1,0:T(1,128)S(1)}, f32[3,3,3,96,96]{4,3,2,1,0:T(8,128)S(1)}, f32[12,4,96,130]{3,2,1,0:T(8,128)}) %tuple.104), branch_computations={%region_18.19_spmd, %region_19.20_spmd} | conditional | flops 3060301824 | bytes 42369572 | solution.py:86
  324.7 17.1 %conditional.18 = (f32[4,2,96,128]{3,2,1,0:T(8,128)}) conditional(s32[]{:T(128)} %convert_element_type.11, () %tuple.88, (f32[1,96]{1,0:T(1,128)S(1)}, f32[12,4,96,130]{3,2,1,0:T(8,128)}, f32[3,3,3,96,96]{4,3,2,1,0:T(8,128)S(1)}) %tuple.89), branch_computations={%region_16.17_spmd, %region_17.18_spmd} | conditional | flops 3060301824 | bytes 117903912 | solution.py:86
  344.5 4.1 collective-permute-start.13
  348.7 20.9 %collective-permute-done.12 = f32[12,1,96,128]{3,2,1,0:T(8,128)S(1)} collective-permute-done((f32[12,1,96,128]{3,2,1,0:T(8,128)S(1)}, f32[12,1,96,128]{3,2,1,0:T(8,128)S(1)}, u32[]{:S(2)}, u32[]{:S(2)}) %collective-permute-start.12) | collective-permute-done | bytes 589856 | tf_op jit(solution)/shard_map/ppermute | solution.py:21
  374.9 3.2 copy.45
  386.8 6.3 %maximum_select_fusion.3 = f32[12,4,96,130]{3,2,1,0:T(8,128)} fusion(f32[12,4,96,1]{3,2,1,0:T(8,128)} %copy.48, f32[12,1,96,128]{3,2,1,0:T(8,128)} %copy-done.30, f32[12,2,96,128]{3,2,1,0:T(8,128)} %copy-done.21, f32[12,1,96,128]{3,2,1,0:T(8,128)S(1)} %copy-done.29, f32[12,4,96,1]{3,2,1,0:T(8,128)} %copy.47, pred[4,130]{1,0:T(4,128)(4,1)S(1)} %broadcast_and_fusion), kind=kLoop, calls=%fused_computation.1515 | loop fusion | flops 2995200 | bytes 4792840 | tf_op jit(solution)/shard_map/jit(_where)/select_n | solution.py:80
  393.1 21.3 %conditional.23 = (f32[4,2,96,128]{3,2,1,0:T(8,128)S(1)}) conditional(s32[]{:T(128)} %convert_element_type.13, () %tuple.96, (f32[1,96]{1,0:T(1,128)S(1)}, f32[3,3,3,96,96]{4,3,2,1,0:T(8,128)S(1)}, f32[12,4,96,130]{3,2,1,0:T(8,128)}) %tuple.153), branch_computations={%region_27.28_spmd, %region_28.29_spmd} | conditional | flops 3060301824 | bytes 42369572 | solution.py:86
  415.2 21.0 %conditional.22 = (f32[4,2,96,128]{3,2,1,0:T(8,128)S(1)}) conditional(s32[]{:T(128)} %convert_element_type.12, () %tuple.94, (f32[1,96]{1,0:T(1,128)S(1)}, f32[3,3,3,96,96]{4,3,2,1,0:T(8,128)S(1)}, f32[12,4,96,130]{3,2,1,0:T(8,128)}) %tuple.154), branch_computations={%region_25.26_spmd, %region_26.27_spmd} | conditional | flops 3060301824 | bytes 42369572 | solution.py:86
  437.0 17.1 %conditional.21 = (f32[4,2,96,128]{3,2,1,0:T(8,128)}) conditional(s32[]{:T(128)} %convert_element_type.11, () %tuple.87, (f32[1,96]{1,0:T(1,128)S(1)}, f32[12,4,96,130]{3,2,1,0:T(8,128)}, f32[3,3,3,96,96]{4,3,2,1,0:T(8,128)S(1)}) %tuple.155), branch_computations={%region_23.24_spmd, %region_24.25_spmd} | conditional | flops 3060301824 | bytes 117903912 | solution.py:86
  454.2 2.7 fusion.1116
  (467 shorter events, 305.0 us)
Async XLA Ops:
  2.8 7.1 %copy-start.36 = (f32[4,96]{1,0:T(4,128)S(1)}, f32[4,96]{1,0:T(4,128)}, u32[]{:S(2)}) copy-start(f32[4,96]{1,0:T(4,128)} %param.32) | copy-start | bytes 4612
  5.6 26.2 %collective-permute-start = (f32[12,1,96,128]{3,2,1,0:T(8,128)}, f32[12,1,96,128]{3,2,1,0:T(8,128)S(1)}, u32[]{:S(2)}, u32[]{:S(2)}) collective-permute-start(f32[12,1,96,128]{3,2,1,0:T(8,128)} %get-tuple-element.223), channel_id=1, source_target_pairs={{0,2},{2,4},{4,6},{6,8},{8,10},{10,12},{12,14},{14,0},{1,3},{3,5},... | collective-permute-start | bytes 1769480 | tf_op jit(solution)/shard_map/ppermute | solution.py:21
  6.8 26.8 %collective-permute-start.1 = (f32[12,1,96,128]{3,2,1,0:T(8,128)}, f32[12,1,96,128]{3,2,1,0:T(8,128)}, u32[]{:S(2)}, u32[]{:S(2)}) collective-permute-start(f32[12,1,96,128]{3,2,1,0:T(8,128)} %get-tuple-element.224), channel_id=1, source_target_pairs={{2,0},{4,2},{6,4},{8,6},{10,8},{12,10},{14,12},{0,14},{3,1},{5,3},... | collective-permute-start | bytes 1769480 | tf_op jit(solution)/shard_map/ppermute | solution.py:23
  37.9 7.2 %copy-start.38 = (s32[8]{0:T(128)S(1)}, s32[8]{0:T(128)}, u32[]{:S(2)}) copy-start(s32[8]{0:T(128)} %param.30) | copy-start | bytes 100
  43.1 5.6 %collective-permute-start.3 = (f32[12,4,96,1]{2,0,3,1:T(8,128)S(1)}, f32[12,4,96,1]{2,0,3,1:T(8,128)S(1)}, u32[]{:S(2)}, u32[]{:S(2)}) collective-permute-start(f32[12,4,96,1]{2,0,3,1:T(8,128)S(1)} %copy.34), channel_id=1, source_target_pairs={{1,0},{0,1},{3,2},{2,3},{5,4},{4,5},{7,6},{6,7},{9,8},{8,9},{11,10... | collective-permute-start | bytes 55304 | tf_op jit(solution)/shard_map/ppermute | solution.py:23
  45.0 1.5 collective-permute-start.2
  58.6 7.1 %copy-start.3 = (f32[12,4,96,130]{3,2,1,0:T(8,128)S(1)}, f32[12,4,96,130]{3,2,1,0:T(8,128)}, u32[]{:S(2)}) copy-start(f32[12,4,96,130]{3,2,1,0:T(8,128)} %get-tuple-element.141) | copy-start | bytes 7188484 | tf_op jit(solution)/shard_map/cond
  81.0 7.1 %copy-start.4 = (f32[12,4,96,130]{3,2,1,0:T(8,128)S(1)}, f32[12,4,96,130]{3,2,1,0:T(8,128)}, u32[]{:S(2)}) copy-start(f32[12,4,96,130]{3,2,1,0:T(8,128)} %get-tuple-element.138) | copy-start | bytes 7188484 | tf_op jit(solution)/shard_map/cond
  120.9 25.1 %collective-permute-start.4 = (f32[12,1,96,128]{3,2,1,0:T(8,128)S(1)}, f32[12,1,96,128]{3,2,1,0:T(8,128)S(1)}, u32[]{:S(2)}, u32[]{:S(2)}) collective-permute-start(f32[12,1,96,128]{3,2,1,0:T(8,128)S(1)} %get-tuple-element.221), channel_id=1, source_target_pairs={{0,2},{2,4},{4,6},{6,8},{8,10},{10,12},{12,14},{14,0},{1,3},{3,5},... | collective-permute-start | bytes 1769480 | tf_op jit(solution)/shard_map/ppermute | solution.py:21
  121.0 27.0 %collective-permute-start.5 = (f32[12,1,96,128]{3,2,1,0:T(8,128)S(1)}, f32[12,1,96,128]{3,2,1,0:T(8,128)S(1)}, u32[]{:S(2)}, u32[]{:S(2)}) collective-permute-start(f32[12,1,96,128]{3,2,1,0:T(8,128)S(1)} %get-tuple-element.222), channel_id=1, source_target_pairs={{2,0},{4,2},{6,4},{8,6},{10,8},{12,10},{14,12},{0,14},{3,1},{5,3},... | collective-permute-start | bytes 1769480 | tf_op jit(solution)/shard_map/ppermute | solution.py:23
  154.6 4.1 collective-permute-start.6
  158.7 2.3 collective-permute-start.7
  171.0 7.1 %copy-start.6 = (f32[12,4,96,130]{3,2,1,0:T(8,128)S(1)}, f32[12,4,96,130]{3,2,1,0:T(8,128)}, u32[]{:S(2)}) copy-start(f32[12,4,96,130]{3,2,1,0:T(8,128)} %get-tuple-element.150) | copy-start | bytes 7188484 | tf_op jit(solution)/shard_map/cond
  191.6 41.7 %copy-start.22 = (f32[4,2,96,128]{3,2,1,0:T(8,128)}, f32[4,2,96,128]{3,2,1,0:T(8,128)S(1)}, u32[]{:S(2)}) copy-start(f32[4,2,96,128]{3,2,1,0:T(8,128)S(1)} %get-tuple-element.238) | copy-start | bytes 1179652
  191.6 40.4 %copy-start.12 = (f32[12,2,96,128]{3,2,1,0:T(8,128)S(1)}, f32[12,2,96,128]{3,2,1,0:T(8,128)}, u32[]{:S(2)}) copy-start(f32[12,2,96,128]{3,2,1,0:T(8,128)} %param.29) | copy-start | bytes 3538948
  193.3 7.1 %copy-start.7 = (f32[12,4,96,130]{3,2,1,0:T(8,128)S(1)}, f32[12,4,96,130]{3,2,1,0:T(8,128)}, u32[]{:S(2)}) copy-start(f32[12,4,96,130]{3,2,1,0:T(8,128)} %get-tuple-element.147) | copy-start | bytes 7188484 | tf_op jit(solution)/shard_map/cond
  214.2 19.1 %copy-start.24 = (f32[4,2,96,128]{3,2,1,0:T(8,128)}, f32[4,2,96,128]{3,2,1,0:T(8,128)S(1)}, u32[]{:S(2)}) copy-start(f32[4,2,96,128]{3,2,1,0:T(8,128)S(1)} %get-tuple-element.237) | copy-start | bytes 1179652
  233.8 27.1 %copy-start.20 = (f32[12,2,96,128]{3,2,1,0:T(8,128)}, f32[12,2,96,128]{3,2,1,0:T(8,128)S(1)}, u32[]{:S(2)}) copy-start(f32[12,2,96,128]{3,2,1,0:T(8,128)S(1)} %divide_multiply_fusion.1) | copy-start | bytes 3538948
  233.9 25.0 %collective-permute-start.8 = (f32[12,1,96,128]{3,2,1,0:T(8,128)S(1)}, f32[12,1,96,128]{3,2,1,0:T(8,128)S(1)}, u32[]{:S(2)}, u32[]{:S(2)}) collective-permute-start(f32[12,1,96,128]{3,2,1,0:T(8,128)S(1)} %get-tuple-element.219), channel_id=1, source_target_pairs={{0,2},{2,4},{4,6},{6,8},{8,10},{10,12},{12,14},{14,0},{1,3},{3,5},... | collective-permute-start | bytes 1769480 | tf_op jit(solution)/shard_map/ppermute | solution.py:21
  233.9 26.9 %collective-permute-start.9 = (f32[12,1,96,128]{3,2,1,0:T(8,128)S(1)}, f32[12,1,96,128]{3,2,1,0:T(8,128)S(1)}, u32[]{:S(2)}, u32[]{:S(2)}) collective-permute-start(f32[12,1,96,128]{3,2,1,0:T(8,128)S(1)} %get-tuple-element.220), channel_id=1, source_target_pairs={{2,0},{4,2},{6,4},{8,6},{10,8},{12,10},{14,12},{0,14},{3,1},{5,3},... | collective-permute-start | bytes 1769480 | tf_op jit(solution)/shard_map/ppermute | solution.py:23
  267.4 4.2 collective-permute-start.10
  271.6 2.3 collective-permute-start.11
  283.9 6.9 %copy-start.9 = (f32[12,4,96,130]{3,2,1,0:T(8,128)S(1)}, f32[12,4,96,130]{3,2,1,0:T(8,128)}, u32[]{:S(2)}) copy-start(f32[12,4,96,130]{3,2,1,0:T(8,128)} %get-tuple-element.159) | copy-start | bytes 7188484 | tf_op jit(solution)/shard_map/cond
  305.3 6.9 %copy-start.10 = (f32[12,4,96,130]{3,2,1,0:T(8,128)S(1)}, f32[12,4,96,130]{3,2,1,0:T(8,128)}, u32[]{:S(2)}) copy-start(f32[12,4,96,130]{3,2,1,0:T(8,128)} %get-tuple-element.156) | copy-start | bytes 7188484 | tf_op jit(solution)/shard_map/cond
  324.7 18.2 %copy-start.37 = (f32[96]{0:T(128)S(1)}, f32[96]{0:T(128)}, u32[]{:S(2)}) copy-start(f32[96]{0:T(128)} %get-tuple-element.225) | copy-start | bytes 1156
  344.4 27.2 %copy-start.21 = (f32[12,2,96,128]{3,2,1,0:T(8,128)}, f32[12,2,96,128]{3,2,1,0:T(8,128)S(1)}, u32[]{:S(2)}) copy-start(f32[12,2,96,128]{3,2,1,0:T(8,128)S(1)} %divide_multiply_fusion) | copy-start | bytes 3538948
  344.5 25.1 %collective-permute-start.12 = (f32[12,1,96,128]{3,2,1,0:T(8,128)S(1)}, f32[12,1,96,128]{3,2,1,0:T(8,128)S(1)}, u32[]{:S(2)}, u32[]{:S(2)}) collective-permute-start(f32[12,1,96,128]{3,2,1,0:T(8,128)S(1)} %get-tuple-element.217), channel_id=1, source_target_pairs={{0,2},{2,4},{4,6},{6,8},{8,10},{10,12},{12,14},{14,0},{1,3},{3,5},... | collective-permute-start | bytes 1769480 | tf_op jit(solution)/shard_map/ppermute | solution.py:21
  344.5 27.1 %collective-permute-start.13 = (f32[12,1,96,128]{3,2,1,0:T(8,128)S(1)}, f32[12,1,96,128]{3,2,1,0:T(8,128)S(1)}, u32[]{:S(2)}, u32[]{:S(2)}) collective-permute-start(f32[12,1,96,128]{3,2,1,0:T(8,128)S(1)} %get-tuple-element.218), channel_id=1, source_target_pairs={{2,0},{4,2},{6,4},{8,6},{10,8},{12,10},{14,12},{0,14},{3,1},{5,3},... | collective-permute-start | bytes 1769480 | tf_op jit(solution)/shard_map/ppermute | solution.py:23
  379.7 4.9 %collective-permute-start.15 = (f32[12,4,96,1]{2,0,3,1:T(8,128)}, f32[12,4,96,1]{2,0,3,1:T(8,128)S(1)}, u32[]{:S(2)}, u32[]{:S(2)}) collective-permute-start(f32[12,4,96,1]{2,0,3,1:T(8,128)} %copy.46), channel_id=1, source_target_pairs={{1,0},{0,1},{3,2},{2,3},{5,4},{4,5},{7,6},{6,7},{9,8},{8,9},{11,10... | collective-permute-start | bytes 55304 | tf_op jit(solution)/shard_map/ppermute | solution.py:23
  381.0 1.4 collective-permute-start.14
  437.0 17.2 %copy-start.23 = (f32[4,2,96,128]{3,2,1,0:T(8,128)S(1)}, f32[4,2,96,128]{3,2,1,0:T(8,128)}, u32[]{:S(2)}) copy-start(f32[4,2,96,128]{3,2,1,0:T(8,128)} %copy-done.22) | copy-start | bytes 1179652
  437.0 17.2 %copy-start.25 = (f32[4,2,96,128]{3,2,1,0:T(8,128)S(1)}, f32[4,2,96,128]{3,2,1,0:T(8,128)}, u32[]{:S(2)}) copy-start(f32[4,2,96,128]{3,2,1,0:T(8,128)} %copy-done.24) | copy-start | bytes 1179652
  (23 other events, 78.9 us)
where the time goes:
time: 464 us; the launch traced here: 457 us
  matrix products  233 us (50%)
  waiting for transfers between devices  87.9 us (19%)
  local copies, waits for them, and re-layouts  65.8 us (14%)
  other arithmetic  39.2 us (8%)
  starting transfers between devices  23.3 us (5%)
  loops' own time  6.67 us (1%)
    dot_general x324, matrix products, convolve(): jnp.einsum('frcw,dc->frdw', piece, weight[tap_t, tap_y, tap_x], precision...  233 us
    ppermute x8, waiting for transfers between devices, extended(): lax.ppermute(tail, axis, [(i, (i + 1) % count) for i in range(count)])  80 us
    select_n x4, other arithmetic, conv_layer(): wide = jnp.where(keep, wide, 0.0)  24.6 us
    slice x12, local copies, waits for them, and re-layouts, extended(): lax.slice_in_dim(cells, cells.shape[dim] - width, cells.shape[dim], axis=...  23.7 us
    ppermute x8, starting transfers between devices, extended(): lax.ppermute(head, axis, [((i + 1) % count, i) for i in range(count)])  18.8 us
    slice x4, local copies, waits for them, and re-layouts, extended(): head = lax.slice_in_dim(cells, 0, width, axis=dim)  9.37 us
  transfers between devices with their start and end apart: 16, of which 9 were waited for; matrix products, arithmetic and copies ran while one was open for 5% of the time, Pallas kernels for 0%

commit v1 on v0

--- a/solution.py
+++ b/solution.py
@@ -47,7 +47,7 @@
                     "frcw,dc->frdw",
                     piece,
                     weight[tap_t, tap_y, tap_x],
-                    precision=lax.Precision.HIGHEST,
+                    precision=lax.Precision.HIGH,
                 )
     return total
 

time: 464 us -> 415 us (0.89)
  matrix products: 233 us -> 184 us
    dot_general x324, matrix products: 233 us -> 184 us  [convolve(): jnp.einsum('frcw,dc->frdw', piece, weight[tap_t, tap_y, tap_x], precision...]
where the time goes in v1:
time: 415 us; the launch traced here: 408 us
  matrix products  184 us (44%)
  waiting for transfers between devices  87.7 us (21%)
  local copies, waits for them, and re-layouts  66.2 us (16%)
  other arithmetic  39.2 us (9%)
  starting transfers between devices  23.5 us (6%)
  loops' own time  5.76 us (1%)
    dot_general x324, matrix products, convolve(): jnp.einsum('frcw,dc->frdw', piece, weight[tap_t, tap_y, tap_x], precision...  184 us
    ppermute x8, waiting for transfers between devices, extended(): lax.ppermute(tail, axis, [(i, (i + 1) % count) for i in range(count)])  79.7 us
    select_n x4, other arithmetic, conv_layer(): wide = jnp.where(keep, wide, 0.0)  24.6 us
    slice x12, local copies, waits for them, and re-layouts, extended(): lax.slice_in_dim(cells, cells.shape[dim] - width, cells.shape[dim], axis=...  23.7 us
    ppermute x8, starting transfers between devices, extended(): lax.ppermute(head, axis, [((i + 1) % count, i) for i in range(count)])  19 us
    slice x4, local copies, waits for them, and re-layouts, extended(): head = lax.slice_in_dim(cells, 0, width, axis=dim)  9.37 us
    ppermute x4, local copies, waits for them, and re-layouts, extended(): lax.ppermute(tail, axis, [(i, (i + 1) % count) for i in range(count)])  8.8 us
    ppermute x4, local copies, waits for them, and re-layouts, extended(): lax.ppermute(head, axis, [((i + 1) % count, i) for i in range(count)])  8.64 us
  transfers between devices with their start and end apart: 16, of which 9 were waited for; matrix products, arithmetic and copies ran while one was open for 5% of the time, Pallas kernels for 0%

profile of v1, /device:TPU:5, one launch (start us, length us, event | category | flops | bytes accessed | tf_op | source)
XLA Modules:
  0.0 407.9 jit_solution(11445939201305301012)
XLA Ops:
  6.8 3.0 collective-permute-start.1
  10.5 4.6 %slice_bitcast_fusion.3 = (f32[3,3,3,96,96]{4,3,2,1,0:T(8,128)}, f32[3,3,3,96,96]{4,3,2,1,0:T(8,128)}, f32[3,3,3,96,96]{4,3,2,1,0:T(8,128)}, f32[3,3,3,96,96]{4,3,2,1,0:T(8,128)S(1)}) fusion(f32[4,3,3,3,96,96]{5,4,3,2,1,0:T(8,128)} %param.31), kind=kLoop, calls=%fused_computation.1523 | loop fusion | bytes 7962624 | tf_op jit(solution)/shard_map/squeeze | solution.py:95
  15.1 16.7 %collective-permute-done = f32[12,1,96,128]{3,2,1,0:T(8,128)S(1)} collective-permute-done((f32[12,1,96,128]{3,2,1,0:T(8,128)}, f32[12,1,96,128]{3,2,1,0:T(8,128)S(1)}, u32[]{:S(2)}, u32[]{:S(2)}) %collective-permute-start) | collective-permute-done | bytes 589856 | tf_op jit(solution)/shard_map/ppermute | solution.py:21
  34.9 3.0 fusion.1121
  37.9 2.6 copy.33
  40.5 2.6 copy.34
  50.9 6.0 %maximum_select_fusion = f32[12,4,96,130]{3,2,1,0:T(8,128)} fusion(f32[12,4,96,1]{3,2,1,0:T(8,128)} %copy.36, f32[12,1,96,128]{3,2,1,0:T(8,128)} %collective-permute-done.1, f32[12,2,96,128]{3,2,1,0:T(8,128)S(1)} %divide_multiply_fusion.3, f32[12,1,96,128]{3,2,1,0:T(8,128)S(1)} %collective-permute-done, f32[12,4,96,1]{3,2,1,0:T(8,128)} %copy.35, ...), kind=kLoop, calls=%fused_computation.1512 | loop fusion | flops 2995200 | bytes 4792840 | tf_op jit(solution)/shard_map/jit(_where)/select_n | solution.py:80
  56.9 18.0 %conditional.14 = (f32[4,2,96,128]{3,2,1,0:T(8,128)S(1)}) conditional(s32[]{:T(128)} %convert_element_type.13, () %tuple.82, (f32[1,96]{1,0:T(1,128)S(1)}, f32[3,3,3,96,96]{4,3,2,1,0:T(8,128)}, f32[12,4,96,130]{3,2,1,0:T(8,128)}) %tuple.98), branch_computations={%region_6.7_spmd, %region_7.8_spmd} | conditional | flops 1531478016 | bytes 46350784 | solution.py:86
  74.9 18.0 %conditional.13 = (f32[4,2,96,128]{3,2,1,0:T(8,128)S(1)}) conditional(s32[]{:T(128)} %convert_element_type.12, () %tuple.80, (f32[1,96]{1,0:T(1,128)S(1)}, f32[3,3,3,96,96]{4,3,2,1,0:T(8,128)}, f32[12,4,96,130]{3,2,1,0:T(8,128)}) %tuple.98), branch_computations={%region_4.5_spmd, %region_5.6_spmd} | conditional | flops 1531478016 | bytes 46350784 | solution.py:86
  92.9 13.6 %conditional.12 = (f32[4,2,96,128]{3,2,1,0:T(8,128)S(1)}) conditional(s32[]{:T(128)} %convert_element_type.11, () %tuple.78, (f32[1,96]{1,0:T(1,128)S(1)}, f32[12,4,96,130]{3,2,1,0:T(8,128)}, f32[3,3,3,96,96]{4,3,2,1,0:T(8,128)}) %tuple.79), branch_computations={%region_2.3_spmd, %region_3.4_spmd} | conditional | flops 1531478016 | bytes 121885120 | solution.py:86
  108.8 4.1 %collective-permute-start.5 = (f32[12,1,96,128]{3,2,1,0:T(8,128)S(1)}, f32[12,1,96,128]{3,2,1,0:T(8,128)S(1)}, u32[]{:S(2)}, u32[]{:S(2)}) collective-permute-start(f32[12,1,96,128]{3,2,1,0:T(8,128)S(1)} %get-tuple-element.222), channel_id=1, source_target_pairs={{2,0},{4,2},{6,4},{8,6},{10,8},{12,10},{14,12},{0,14},{3,1},{5,3},... | collective-permute-start | bytes 1769480 | tf_op jit(solution)/shard_map/ppermute | solution.py:23
  113.0 20.9 %collective-permute-done.4 = f32[12,1,96,128]{3,2,1,0:T(8,128)S(1)} collective-permute-done((f32[12,1,96,128]{3,2,1,0:T(8,128)S(1)}, f32[12,1,96,128]{3,2,1,0:T(8,128)S(1)}, u32[]{:S(2)}, u32[]{:S(2)}) %collective-permute-start.4) | collective-permute-done | bytes 589856 | tf_op jit(solution)/shard_map/ppermute | solution.py:21
  136.8 3.0 fusion.1120
  150.9 6.0 %maximum_select_fusion.1 = f32[12,4,96,130]{3,2,1,0:T(8,128)} fusion(f32[12,4,96,1]{3,2,1,0:T(8,128)} %copy.40, f32[12,1,96,128]{3,2,1,0:T(8,128)} %copy-done.31, f32[12,2,96,128]{3,2,1,0:T(8,128)S(1)} %divide_multiply_fusion.2, f32[12,1,96,128]{3,2,1,0:T(8,128)S(1)} %collective-permute-done.4, f32[12,4,96,1]{3,2,1,0:T(8,128)} %copy.39, ...), kind=kLoop, calls=%fused_computation.1513 | loop fusion | flops 2995200 | bytes 4792840 | tf_op jit(solution)/shard_map/jit(_where)/select_n | solution.py:80
  156.9 18.0 %conditional.17 = (f32[4,2,96,128]{3,2,1,0:T(8,128)S(1)}) conditional(s32[]{:T(128)} %convert_element_type.13, () %tuple.86, (f32[1,96]{1,0:T(1,128)S(1)}, f32[3,3,3,96,96]{4,3,2,1,0:T(8,128)}, f32[12,4,96,130]{3,2,1,0:T(8,128)}) %tuple.101), branch_computations={%region_13.14_spmd, %region_14.15_spmd} | conditional | flops 1531478016 | bytes 46350784 | solution.py:86
  174.9 18.3 %conditional.16 = (f32[4,2,96,128]{3,2,1,0:T(8,128)S(1)}) conditional(s32[]{:T(128)} %convert_element_type.12, () %tuple.84, (f32[1,96]{1,0:T(1,128)S(1)}, f32[3,3,3,96,96]{4,3,2,1,0:T(8,128)}, f32[12,4,96,130]{3,2,1,0:T(8,128)}) %tuple.101), branch_computations={%region_11.12_spmd, %region_12.13_spmd} | conditional | flops 1531478016 | bytes 46350784 | solution.py:86
  193.2 14.3 %conditional.15 = (f32[4,2,96,128]{3,2,1,0:T(8,128)}) conditional(s32[]{:T(128)} %convert_element_type.11, () %tuple.77, (f32[1,96]{1,0:T(1,128)S(1)}, f32[12,4,96,130]{3,2,1,0:T(8,128)}, f32[3,3,3,96,96]{4,3,2,1,0:T(8,128)}) %tuple.83), branch_computations={%region_9.10_spmd, %region_10.11_spmd} | conditional | flops 1531478016 | bytes 121885120 | solution.py:86
  209.5 4.1 %collective-permute-start.9 = (f32[12,1,96,128]{3,2,1,0:T(8,128)S(1)}, f32[12,1,96,128]{3,2,1,0:T(8,128)S(1)}, u32[]{:S(2)}, u32[]{:S(2)}) collective-permute-start(f32[12,1,96,128]{3,2,1,0:T(8,128)S(1)} %get-tuple-element.220), channel_id=1, source_target_pairs={{2,0},{4,2},{6,4},{8,6},{10,8},{12,10},{14,12},{0,14},{3,1},{5,3},... | collective-permute-start | bytes 1769480 | tf_op jit(solution)/shard_map/ppermute | solution.py:23
  213.7 20.7 %collective-permute-done.8 = f32[12,1,96,128]{3,2,1,0:T(8,128)S(1)} collective-permute-done((f32[12,1,96,128]{3,2,1,0:T(8,128)S(1)}, f32[12,1,96,128]{3,2,1,0:T(8,128)S(1)}, u32[]{:S(2)}, u32[]{:S(2)}) %collective-permute-start.8) | collective-permute-done | bytes 589856 | tf_op jit(solution)/shard_map/ppermute | solution.py:21
  237.4 3.0 fusion.1119
  251.6 6.2 %maximum_select_fusion.2 = f32[12,4,96,130]{3,2,1,0:T(8,128)} fusion(f32[12,4,96,1]{3,2,1,0:T(8,128)} %copy.44, f32[12,1,96,128]{3,2,1,0:T(8,128)} %copy-done.32, f32[12,2,96,128]{3,2,1,0:T(8,128)} %copy-done.20, f32[12,1,96,128]{3,2,1,0:T(8,128)S(1)} %collective-permute-done.8, f32[12,4,96,1]{3,2,1,0:T(8,128)} %copy.43, ...), kind=kLoop, calls=%fused_computation.1514 | loop fusion | flops 2995200 | bytes 4792840 | tf_op jit(solution)/shard_map/jit(_where)/select_n | solution.py:80
  257.8 17.0 %conditional.20 = (f32[4,2,96,128]{3,2,1,0:T(8,128)S(1)}) conditional(s32[]{:T(128)} %convert_element_type.13, () %tuple.92, (f32[1,96]{1,0:T(1,128)S(1)}, f32[3,3,3,96,96]{4,3,2,1,0:T(8,128)S(1)}, f32[12,4,96,130]{3,2,1,0:T(8,128)}) %tuple.104), branch_computations={%region_20.21_spmd, %region_21.22_spmd} | conditional | flops 1531478016 | bytes 42369572 | solution.py:86
  274.8 17.0 %conditional.19 = (f32[4,2,96,128]{3,2,1,0:T(8,128)S(1)}) conditional(s32[]{:T(128)} %convert_element_type.12, () %tuple.90, (f32[1,96]{1,0:T(1,128)S(1)}, f32[3,3,3,96,96]{4,3,2,1,0:T(8,128)S(1)}, f32[12,4,96,130]{3,2,1,0:T(8,128)}) %tuple.104), branch_computations={%region_18.19_spmd, %region_19.20_spmd} | conditional | flops 1531478016 | bytes 42369572 | solution.py:86
  291.9 13.2 %conditional.18 = (f32[4,2,96,128]{3,2,1,0:T(8,128)}) conditional(s32[]{:T(128)} %convert_element_type.11, () %tuple.88, (f32[1,96]{1,0:T(1,128)S(1)}, f32[12,4,96,130]{3,2,1,0:T(8,128)}, f32[3,3,3,96,96]{4,3,2,1,0:T(8,128)S(1)}) %tuple.89), branch_computations={%region_16.17_spmd, %region_17.18_spmd} | conditional | flops 1531478016 | bytes 117903912 | solution.py:86
  307.8 4.1 %collective-permute-start.13 = (f32[12,1,96,128]{3,2,1,0:T(8,128)S(1)}, f32[12,1,96,128]{3,2,1,0:T(8,128)S(1)}, u32[]{:S(2)}, u32[]{:S(2)}) collective-permute-start(f32[12,1,96,128]{3,2,1,0:T(8,128)S(1)} %get-tuple-element.218), channel_id=1, source_target_pairs={{2,0},{4,2},{6,4},{8,6},{10,8},{12,10},{14,12},{0,14},{3,1},{5,3},... | collective-permute-start | bytes 1769480 | tf_op jit(solution)/shard_map/ppermute | solution.py:23
  311.9 20.7 %collective-permute-done.12 = f32[12,1,96,128]{3,2,1,0:T(8,128)S(1)} collective-permute-done((f32[12,1,96,128]{3,2,1,0:T(8,128)S(1)}, f32[12,1,96,128]{3,2,1,0:T(8,128)S(1)}, u32[]{:S(2)}, u32[]{:S(2)}) %collective-permute-start.12) | collective-permute-done | bytes 589856 | tf_op jit(solution)/shard_map/ppermute | solution.py:21
  337.9 3.2 copy.45
  350.0 6.3 %maximum_select_fusion.3 = f32[12,4,96,130]{3,2,1,0:T(8,128)} fusion(f32[12,4,96,1]{3,2,1,0:T(8,128)} %copy.48, f32[12,1,96,128]{3,2,1,0:T(8,128)} %copy-done.30, f32[12,2,96,128]{3,2,1,0:T(8,128)} %copy-done.21, f32[12,1,96,128]{3,2,1,0:T(8,128)S(1)} %copy-done.29, f32[12,4,96,1]{3,2,1,0:T(8,128)} %copy.47, pred[4,130]{1,0:T(4,128)(4,1)S(1)} %broadcast_and_fusion), kind=kLoop, calls=%fused_computation.1515 | loop fusion | flops 2995200 | bytes 4792840 | tf_op jit(solution)/shard_map/jit(_where)/select_n | solution.py:80
  356.4 17.0 %conditional.23 = (f32[4,2,96,128]{3,2,1,0:T(8,128)S(1)}) conditional(s32[]{:T(128)} %convert_element_type.13, () %tuple.96, (f32[1,96]{1,0:T(1,128)S(1)}, f32[3,3,3,96,96]{4,3,2,1,0:T(8,128)S(1)}, f32[12,4,96,130]{3,2,1,0:T(8,128)}) %tuple.153), branch_computations={%region_27.28_spmd, %region_28.29_spmd} | conditional | flops 1531478016 | bytes 42369572 | solution.py:86
  374.1 17.0 %conditional.22 = (f32[4,2,96,128]{3,2,1,0:T(8,128)S(1)}) conditional(s32[]{:T(128)} %convert_element_type.12, () %tuple.94, (f32[1,96]{1,0:T(1,128)S(1)}, f32[3,3,3,96,96]{4,3,2,1,0:T(8,128)S(1)}, f32[12,4,96,130]{3,2,1,0:T(8,128)}) %tuple.154), branch_computations={%region_25.26_spmd, %region_26.27_spmd} | conditional | flops 1531478016 | bytes 42369572 | solution.py:86
  391.9 13.1 %conditional.21 = (f32[4,2,96,128]{3,2,1,0:T(8,128)}) conditional(s32[]{:T(128)} %convert_element_type.11, () %tuple.87, (f32[1,96]{1,0:T(1,128)S(1)}, f32[12,4,96,130]{3,2,1,0:T(8,128)}, f32[3,3,3,96,96]{4,3,2,1,0:T(8,128)S(1)}) %tuple.155), branch_computations={%region_23.24_spmd, %region_24.25_spmd} | conditional | flops 1531478016 | bytes 117903912 | solution.py:86
  405.0 2.7 fusion.1116
  (467 shorter events, 256.9 us)
Async XLA Ops:
  2.8 7.1 %copy-start.36 = (f32[4,96]{1,0:T(4,128)S(1)}, f32[4,96]{1,0:T(4,128)}, u32[]{:S(2)}) copy-start(f32[4,96]{1,0:T(4,128)} %param.32) | copy-start | bytes 4612
  5.6 26.2 %collective-permute-start = (f32[12,1,96,128]{3,2,1,0:T(8,128)}, f32[12,1,96,128]{3,2,1,0:T(8,128)S(1)}, u32[]{:S(2)}, u32[]{:S(2)}) collective-permute-start(f32[12,1,96,128]{3,2,1,0:T(8,128)} %get-tuple-element.223), channel_id=1, source_target_pairs={{0,2},{2,4},{4,6},{6,8},{8,10},{10,12},{12,14},{14,0},{1,3},{3,5},... | collective-permute-start | bytes 1769480 | tf_op jit(solution)/shard_map/ppermute | solution.py:21
  6.8 26.8 %collective-permute-start.1 = (f32[12,1,96,128]{3,2,1,0:T(8,128)}, f32[12,1,96,128]{3,2,1,0:T(8,128)}, u32[]{:S(2)}, u32[]{:S(2)}) collective-permute-start(f32[12,1,96,128]{3,2,1,0:T(8,128)} %get-tuple-element.224), channel_id=1, source_target_pairs={{2,0},{4,2},{6,4},{8,6},{10,8},{12,10},{14,12},{0,14},{3,1},{5,3},... | collective-permute-start | bytes 1769480 | tf_op jit(solution)/shard_map/ppermute | solution.py:23
  37.9 7.2 %copy-start.38 = (s32[8]{0:T(128)S(1)}, s32[8]{0:T(128)}, u32[]{:S(2)}) copy-start(s32[8]{0:T(128)} %param.30) | copy-start | bytes 100
  43.1 5.6 %collective-permute-start.3 = (f32[12,4,96,1]{2,0,3,1:T(8,128)S(1)}, f32[12,4,96,1]{2,0,3,1:T(8,128)S(1)}, u32[]{:S(2)}, u32[]{:S(2)}) collective-permute-start(f32[12,4,96,1]{2,0,3,1:T(8,128)S(1)} %copy.34), channel_id=1, source_target_pairs={{1,0},{0,1},{3,2},{2,3},{5,4},{4,5},{7,6},{6,7},{9,8},{8,9},{11,10... | collective-permute-start | bytes 55304 | tf_op jit(solution)/shard_map/ppermute | solution.py:23
  45.0 1.5 collective-permute-start.2
  58.5 6.5 %copy-start.3 = (f32[12,4,96,130]{3,2,1,0:T(8,128)S(1)}, f32[12,4,96,130]{3,2,1,0:T(8,128)}, u32[]{:S(2)}) copy-start(f32[12,4,96,130]{3,2,1,0:T(8,128)} %get-tuple-element.141) | copy-start | bytes 7188484 | tf_op jit(solution)/shard_map/cond
  76.5 6.5 %copy-start.4 = (f32[12,4,96,130]{3,2,1,0:T(8,128)S(1)}, f32[12,4,96,130]{3,2,1,0:T(8,128)}, u32[]{:S(2)}) copy-start(f32[12,4,96,130]{3,2,1,0:T(8,128)} %get-tuple-element.138) | copy-start | bytes 7188484 | tf_op jit(solution)/shard_map/cond
  108.7 25.1 %collective-permute-start.4 = (f32[12,1,96,128]{3,2,1,0:T(8,128)S(1)}, f32[12,1,96,128]{3,2,1,0:T(8,128)S(1)}, u32[]{:S(2)}, u32[]{:S(2)}) collective-permute-start(f32[12,1,96,128]{3,2,1,0:T(8,128)S(1)} %get-tuple-element.221), channel_id=1, source_target_pairs={{0,2},{2,4},{4,6},{6,8},{8,10},{10,12},{12,14},{14,0},{1,3},{3,5},... | collective-permute-start | bytes 1769480 | tf_op jit(solution)/shard_map/ppermute | solution.py:21
  108.8 27.0 %collective-permute-start.5 = (f32[12,1,96,128]{3,2,1,0:T(8,128)S(1)}, f32[12,1,96,128]{3,2,1,0:T(8,128)S(1)}, u32[]{:S(2)}, u32[]{:S(2)}) collective-permute-start(f32[12,1,96,128]{3,2,1,0:T(8,128)S(1)} %get-tuple-element.222), channel_id=1, source_target_pairs={{2,0},{4,2},{6,4},{8,6},{10,8},{12,10},{14,12},{0,14},{3,1},{5,3},... | collective-permute-start | bytes 1769480 | tf_op jit(solution)/shard_map/ppermute | solution.py:23
  142.4 4.1 %collective-permute-start.6 = (f32[12,4,96,1]{2,0,3,1:T(8,128)S(1)}, f32[12,4,96,1]{2,0,3,1:T(8,128)S(1)}, u32[]{:S(2)}, u32[]{:S(2)}) collective-permute-start(f32[12,4,96,1]{2,0,3,1:T(8,128)S(1)} %copy.37), channel_id=1, source_target_pairs={{0,1},{1,0},{2,3},{3,2},{4,5},{5,4},{6,7},{7,6},{8,9},{9,8},{10,11... | collective-permute-start | bytes 55304 | tf_op jit(solution)/shard_map/ppermute | solution.py:21
  146.5 2.3 collective-permute-start.7
  158.5 6.5 %copy-start.6 = (f32[12,4,96,130]{3,2,1,0:T(8,128)S(1)}, f32[12,4,96,130]{3,2,1,0:T(8,128)}, u32[]{:S(2)}) copy-start(f32[12,4,96,130]{3,2,1,0:T(8,128)} %get-tuple-element.150) | copy-start | bytes 7188484 | tf_op jit(solution)/shard_map/cond
  174.9 34.0 %copy-start.22 = (f32[4,2,96,128]{3,2,1,0:T(8,128)}, f32[4,2,96,128]{3,2,1,0:T(8,128)S(1)}, u32[]{:S(2)}) copy-start(f32[4,2,96,128]{3,2,1,0:T(8,128)S(1)} %get-tuple-element.238) | copy-start | bytes 1179652
  174.9 32.7 %copy-start.12 = (f32[12,2,96,128]{3,2,1,0:T(8,128)S(1)}, f32[12,2,96,128]{3,2,1,0:T(8,128)}, u32[]{:S(2)}) copy-start(f32[12,2,96,128]{3,2,1,0:T(8,128)} %param.29) | copy-start | bytes 3538948
  176.8 6.5 %copy-start.7 = (f32[12,4,96,130]{3,2,1,0:T(8,128)S(1)}, f32[12,4,96,130]{3,2,1,0:T(8,128)}, u32[]{:S(2)}) copy-start(f32[12,4,96,130]{3,2,1,0:T(8,128)} %get-tuple-element.147) | copy-start | bytes 7188484 | tf_op jit(solution)/shard_map/cond
  193.2 15.7 %copy-start.24 = (f32[4,2,96,128]{3,2,1,0:T(8,128)}, f32[4,2,96,128]{3,2,1,0:T(8,128)S(1)}, u32[]{:S(2)}) copy-start(f32[4,2,96,128]{3,2,1,0:T(8,128)S(1)} %get-tuple-element.237) | copy-start | bytes 1179652
  209.4 27.1 %copy-start.20 = (f32[12,2,96,128]{3,2,1,0:T(8,128)}, f32[12,2,96,128]{3,2,1,0:T(8,128)S(1)}, u32[]{:S(2)}) copy-start(f32[12,2,96,128]{3,2,1,0:T(8,128)S(1)} %divide_multiply_fusion.1) | copy-start | bytes 3538948
  209.4 25.0 %collective-permute-start.8 = (f32[12,1,96,128]{3,2,1,0:T(8,128)S(1)}, f32[12,1,96,128]{3,2,1,0:T(8,128)S(1)}, u32[]{:S(2)}, u32[]{:S(2)}) collective-permute-start(f32[12,1,96,128]{3,2,1,0:T(8,128)S(1)} %get-tuple-element.219), channel_id=1, source_target_pairs={{0,2},{2,4},{4,6},{6,8},{8,10},{10,12},{12,14},{14,0},{1,3},{3,5},... | collective-permute-start | bytes 1769480 | tf_op jit(solution)/shard_map/ppermute | solution.py:21
  209.5 26.9 %collective-permute-start.9 = (f32[12,1,96,128]{3,2,1,0:T(8,128)S(1)}, f32[12,1,96,128]{3,2,1,0:T(8,128)S(1)}, u32[]{:S(2)}, u32[]{:S(2)}) collective-permute-start(f32[12,1,96,128]{3,2,1,0:T(8,128)S(1)} %get-tuple-element.220), channel_id=1, source_target_pairs={{2,0},{4,2},{6,4},{8,6},{10,8},{12,10},{14,12},{0,14},{3,1},{5,3},... | collective-permute-start | bytes 1769480 | tf_op jit(solution)/shard_map/ppermute | solution.py:23
  243.0 4.2 %collective-permute-start.10 = (f32[12,4,96,1]{2,0,3,1:T(8,128)S(1)}, f32[12,4,96,1]{2,0,3,1:T(8,128)S(1)}, u32[]{:S(2)}, u32[]{:S(2)}) collective-permute-start(f32[12,4,96,1]{2,0,3,1:T(8,128)S(1)} %copy.41), channel_id=1, source_target_pairs={{0,1},{1,0},{2,3},{3,2},{4,5},{5,4},{6,7},{7,6},{8,9},{9,8},{10,11... | collective-permute-start | bytes 55304 | tf_op jit(solution)/shard_map/ppermute | solution.py:21
  247.2 2.3 collective-permute-start.11
  291.8 14.4 %copy-start.37 = (f32[96]{0:T(128)S(1)}, f32[96]{0:T(128)}, u32[]{:S(2)}) copy-start(f32[96]{0:T(128)} %get-tuple-element.225) | copy-start | bytes 1156
  307.6 27.1 %copy-start.21 = (f32[12,2,96,128]{3,2,1,0:T(8,128)}, f32[12,2,96,128]{3,2,1,0:T(8,128)S(1)}, u32[]{:S(2)}) copy-start(f32[12,2,96,128]{3,2,1,0:T(8,128)S(1)} %divide_multiply_fusion) | copy-start | bytes 3538948
  307.7 24.9 %collective-permute-start.12 = (f32[12,1,96,128]{3,2,1,0:T(8,128)S(1)}, f32[12,1,96,128]{3,2,1,0:T(8,128)S(1)}, u32[]{:S(2)}, u32[]{:S(2)}) collective-permute-start(f32[12,1,96,128]{3,2,1,0:T(8,128)S(1)} %get-tuple-element.217), channel_id=1, source_target_pairs={{0,2},{2,4},{4,6},{6,8},{8,10},{10,12},{12,14},{14,0},{1,3},{3,5},... | collective-permute-start | bytes 1769480 | tf_op jit(solution)/shard_map/ppermute | solution.py:21
  307.8 26.9 %collective-permute-start.13 = (f32[12,1,96,128]{3,2,1,0:T(8,128)S(1)}, f32[12,1,96,128]{3,2,1,0:T(8,128)S(1)}, u32[]{:S(2)}, u32[]{:S(2)}) collective-permute-start(f32[12,1,96,128]{3,2,1,0:T(8,128)S(1)} %get-tuple-element.218), channel_id=1, source_target_pairs={{2,0},{4,2},{6,4},{8,6},{10,8},{12,10},{14,12},{0,14},{3,1},{5,3},... | collective-permute-start | bytes 1769480 | tf_op jit(solution)/shard_map/ppermute | solution.py:23
  342.7 5.1 %collective-permute-start.15 = (f32[12,4,96,1]{2,0,3,1:T(8,128)}, f32[12,4,96,1]{2,0,3,1:T(8,128)S(1)}, u32[]{:S(2)}, u32[]{:S(2)}) collective-permute-start(f32[12,4,96,1]{2,0,3,1:T(8,128)} %copy.46), channel_id=1, source_target_pairs={{1,0},{0,1},{3,2},{2,3},{5,4},{4,5},{7,6},{6,7},{9,8},{8,9},{11,10... | collective-permute-start | bytes 55304 | tf_op jit(solution)/shard_map/ppermute | solution.py:23
  344.3 1.4 collective-permute-start.14
  350.0 6.3 %copy-start.13 = (f32[3,3,3,96,96]{4,3,2,1,0:T(8,128)S(1)}, f32[3,3,3,96,96]{4,3,2,1,0:T(8,128)}, u32[]{:S(2)}) copy-start(f32[3,3,3,96,96]{4,3,2,1,0:T(8,128)} %get-tuple-element.207) | copy-start | bytes 2985988
  350.0 6.3 %copy-start.35 = (f32[1,96]{1,0:T(1,128)S(1)}, f32[1,96]{1,0:T(1,128)}, u32[]{:S(2)}) copy-start(f32[1,96]{1,0:T(1,128)} %get-tuple-element.232) | copy-start | bytes 1156
  391.9 13.1 %copy-start.23 = (f32[4,2,96,128]{3,2,1,0:T(8,128)S(1)}, f32[4,2,96,128]{3,2,1,0:T(8,128)}, u32[]{:S(2)}) copy-start(f32[4,2,96,128]{3,2,1,0:T(8,128)} %copy-done.22) | copy-start | bytes 1179652
  391.9 13.1 %copy-start.25 = (f32[4,2,96,128]{3,2,1,0:T(8,128)S(1)}, f32[4,2,96,128]{3,2,1,0:T(8,128)}, u32[]{:S(2)}) copy-start(f32[4,2,96,128]{3,2,1,0:T(8,128)} %copy-done.24) | copy-start | bytes 1179652
  (23 other events, 74.8 us)
